TPU v7x, 32 devices: a whole 2x2x4 slice. The times are simulated.
32 devices in a mesh: sensor: 8 (over z, y), param: 4 (over x, core).
Axes of the slice: x: 2, y: 2, z: 4, core: 2. Of those that a mesh axis runs over, the one named last changes fastest.
Arguments:
- parameter_field: float32 [8, 192, 420], P(None, ('param', 'sensor')), may hold values from -6 to 6
- operator_blocks: float32 [2, 421, 8, 4, 384], P(None, None, 'sensor', 'param'), may hold values from -0.625 to 0.625
- noise_weights: float32 [64, 420], P('sensor'), may hold values from 0.25 to 4
Outputs:
- hessian_action: float32 [8, 192, 420], P(None, ('param', 'sensor'))
All inputs are finite; a program needn't handle non-finite values.
Results may differ from a plain program's by a relative error of at most 0.000071.
Values sent between devices are 32-bit elements; how exact they have to be, the bound alone decides.
A program may use at most 64 MiB of HBM per device.

v0:
```python
import functools
import math

import jax
import jax.numpy as jnp
import ml_dtypes
import numpy as np
from jax import lax
from jax.experimental import pallas as pl
from jax.experimental.pallas import tpu as pltpu
from jax.sharding import PartitionSpec as P

LANES = 128
f32 = jnp.float32
bf16 = jnp.bfloat16


def round_up(value, step):
    return -(-value // step) * step


def split_table(table):
    high = table.astype(ml_dtypes.bfloat16)
    low = (table - high.astype(np.float64)).astype(ml_dtypes.bfloat16)
    return np.stack([high, low])


def tables(time_steps):
    length = 2 * time_steps
    freq_count = time_steps + 1
    time_pad = round_up(time_steps, LANES)
    freq_pad = round_up(freq_count, LANES)
    angles = (np.arange(time_steps)[:, None] * np.arange(freq_count)[None, :] % length) * (
        2.0 * math.pi / length
    )
    factor = np.full(freq_count, 2.0)
    factor[0] = factor[-1] = 1.0
    factor /= length
    forward = np.zeros((time_pad, 2 * freq_pad))
    forward[:time_steps, :freq_count] = np.cos(angles)
    forward[:time_steps, freq_pad : freq_pad + freq_count] = -np.sin(angles)
    inverse = np.zeros((2 * freq_pad, time_pad))
    inverse[:freq_count, :time_steps] = factor[:, None] * np.cos(angles).T
    inverse[freq_pad : freq_pad + freq_count, :time_steps] = -factor[:, None] * np.sin(angles).T
    return split_table(forward), split_table(inverse)


def product(left, table_ref, depth):
    high = left.astype(bf16)
    low = (left - high.astype(f32)).astype(bf16)
    table_high = table_ref[0, :depth]
    table_low = table_ref[1, :depth]

    def dot(a, b):
        return jnp.dot(a, b, preferred_element_type=f32)

    return dot(low, table_high) + dot(high, table_low) + dot(high, table_high)


def kernel(
    sizes,
    x_ref,
    blocks_ref,
    weights_ref,
    fwd_hbm,
    inv_hbm,
    out_ref,
    raw,
    ft,
    fwd,
    inv,
    xg,
    xs,
    ps,
    part,
    part_in,
    wexp,
    wdat,
    gs,
    gout,
    y_in,
    z_out,
    z_in,
    local_sem,
    gz_s,
    gz_r,
    gy_s,
    gy_r,
    ps_s,
    ps_r,
    pg_s,
    pg_r,
    ry_s,
    ry_r,
    rz_s,
    rz_r,
):
    vecs, own_pars, steps, sens, pars, n_sensor, n_param, fast = sizes
    slow = n_sensor // fast
    freqs = steps + 1
    freq_pad = round_up(freqs, LANES)
    tiles = freq_pad // LANES
    group_pars = fast * own_pars
    chunk = own_pars * vecs
    group_rows = group_pars * vecs
    rows = sens * vecs
    share = rows // n_param
    unroll = 4 if group_pars % 4 == 0 else 1

    me = lax.axis_index("sensor")
    mp = lax.axis_index("param")
    mz = me // fast
    my = me % fast
    y_peer = mz * fast + (1 - my)

    def z_at(distance):
        return lax.rem(mz + distance, slow)

    def z_back(distance):
        return lax.rem(mz + slow - distance, slow)

    def p_at(distance):
        return lax.rem(mp + distance, n_param)

    def p_back(distance):
        return lax.rem(mp + n_param - distance, n_param)

    def to_sensor(target, src, dst, send, recv):
        return pltpu.make_async_remote_copy(
            src_ref=src, dst_ref=dst, send_sem=send, recv_sem=recv,
            device_id=(target, mp), device_id_type=pl.DeviceIdType.MESH,
        )

    def to_param(target, src, dst, send, recv):
        return pltpu.make_async_remote_copy(
            src_ref=src, dst_ref=dst, send_sem=send, recv_sem=recv,
            device_id=(me, target), device_id_type=pl.DeviceIdType.MESH,
        )

    barrier = pltpu.get_barrier_semaphore()

    def greet(device):
        pl.semaphore_signal(barrier, inc=1, device_id=device, device_id_type=pl.DeviceIdType.MESH)

    greet((y_peer, mp))
    for d in range(1, slow):
        greet((z_at(d) * fast + my, mp))
    for j in range(1, n_param):
        greet((me, p_at(j)))

    blocks_rows = blocks_ref.shape[0]
    load_blocks = pltpu.make_async_copy(
        blocks_ref.at[:, 0], raw.at[pl.ds(0, blocks_rows)], local_sem.at[0]
    )
    load_blocks.start()
    load_fwd = pltpu.make_async_copy(fwd_hbm, fwd, local_sem.at[1])
    load_fwd.start()
    load_inv = pltpu.make_async_copy(inv_hbm, inv, local_sem.at[2])
    load_inv.start()
    pl.semaphore_wait(barrier, 1 + (slow - 1) + (n_param - 1))

    own_y = to_sensor(y_peer, x_ref, xg.at[me], gy_s.at[0], gy_r.at[0])
    own_y.start()
    own_z = {}
    for d in range(1, slow):
        own_z[d] = to_sensor(z_at(d) * fast + my, x_ref, xg.at[me], gz_s.at[d], gz_r.at[d])
        own_z[d].start()

    xg[me] = x_ref[...]
    spread = jnp.concatenate(
        [jnp.broadcast_to(weights_ref[r : r + 1], (vecs, steps)) for r in range(sens)], axis=0
    )
    for i in range(n_param):
        wexp[i] = spread[i * share : (i + 1) * share]

    def turn(part_index, tile):
        width_tiles = (pars * sens) // LANES
        first = pl.multiple_of(tile * LANES, LANES)
        inside = first + lax.broadcasted_iota(jnp.int32, (LANES, LANES), 1) < freqs
        for w in range(width_tiles):
            start = (part_index * freqs + first) * width_tiles + w
            block = raw[pl.ds(start, LANES, stride=width_tiles), :]
            turned = jnp.where(inside, block.T, 0.0)
            per = LANES // sens
            ft[part_index, w * per : (w + 1) * per, :, pl.ds(first, LANES)] = turned.reshape(
                per, sens, LANES
            )

    forwards = {}

    def forward_chunk(d):
        own_z[d].wait_recv()
        source = z_back(d) * fast + my
        forwards[d] = to_sensor(y_peer, xg.at[source], xg.at[source], gy_s.at[d], gy_r.at[d])
        forwards[d].start()

    load_blocks.wait()

    def turn_tile(tile, carry):
        turn(0, tile)
        turn(1, tile)
        return carry

    ready = [d for d in range(1, slow)]
    half = max(tiles // 2, 1)
    lax.fori_loop(0, half, turn_tile, 0)
    for d in ready[:1]:
        forward_chunk(d)
    lax.fori_loop(half, tiles, turn_tile, 0)
    for d in ready[1:]:
        forward_chunk(d)
    load_fwd.wait()

    def lanes_of(tile, c):
        return pl.ds(pl.multiple_of(tile * LANES + c * freq_pad, LANES), LANES)

    def forward_group(zz, initial):
        field = xg[pl.ds(zz * fast, fast)].reshape(group_rows, steps)
        xs[...] = product(field, fwd, steps).reshape(group_pars, vecs, 2 * freq_pad)
        base = zz * group_pars

        def tile_step(tile, carry):
            re, im = lanes_of(tile, 0), lanes_of(tile, 1)
            if initial:
                acc = tuple(jnp.zeros((vecs, LANES), f32) for _ in range(2 * sens))
            else:
                acc = tuple(ps[r, :, re] for r in range(sens)) + tuple(
                    ps[r, :, im] for r in range(sens)
                )

            def par_step(step, acc):
                acc = list(acc)
                for u in range(unroll):
                    q = step * unroll + u
                    xr, xi = xs[q, :, re], xs[q, :, im]
                    for r in range(sens):
                        fr = ft[0, base + q, r : r + 1, re]
                        fi = ft[1, base + q, r : r + 1, re]
                        acc[r] = acc[r] + fr * xr - fi * xi
                        acc[sens + r] = acc[sens + r] + fr * xi + fi * xr
                return tuple(acc)

            acc = lax.fori_loop(0, group_pars // unroll, par_step, acc)
            for r in range(sens):
                ps[r, :, re] = acc[r]
                ps[r, :, im] = acc[sens + r]
            return carry

        lax.fori_loop(0, tiles, tile_step, 0)

    for d in range(slow):
        if d == 0:
            own_y.wait_recv()
        else:
            forwards[d].wait_recv()
        forward_group(z_back(d), d == 0)

    load_inv.wait()
    series = product(ps[...].reshape(rows, 2 * freq_pad), inv, 2 * freq_pad)
    for i in range(n_param):
        part[i] = series[i * share : (i + 1) * share, :steps]
    sums = {}
    for j in range(1, n_param):
        sums[j] = to_param(p_at(j), part.at[p_at(j)], part_in.at[j], ps_s.at[j], ps_r.at[j])
        sums[j].start()
    total = part[mp]
    for j in range(1, n_param):
        sums[j].wait_recv()
        total = total + part_in[j]
    wdat[mp] = total * wexp[mp]
    spreads = {}
    for j in range(1, n_param):
        spreads[j] = to_param(p_at(j), wdat.at[mp], wdat.at[mp], pg_s.at[j], pg_r.at[j])
        spreads[j].start()
    for j in range(1, n_param):
        spreads[j].wait_recv()
    weighted = jnp.concatenate([wdat[i] for i in range(n_param)], axis=0)
    ps[...] = product(weighted, fwd, steps).reshape(sens, vecs, 2 * freq_pad)

    def adjoint_group(zz, slot):
        base = zz * group_pars

        def tile_step(tile, carry):
            re, im = lanes_of(tile, 0), lanes_of(tile, 1)
            wr = [ps[r, :, re] for r in range(sens)]
            wi = [ps[r, :, im] for r in range(sens)]

            def par_step(step, carry):
                for u in range(unroll):
                    q = step * unroll + u
                    gr = jnp.zeros((vecs, LANES), f32)
                    gi = jnp.zeros((vecs, LANES), f32)
                    for r in range(sens):
                        fr = ft[0, base + q, r : r + 1, re]
                        fi = ft[1, base + q, r : r + 1, re]
                        gr = gr + fr * wr[r] + fi * wi[r]
                        gi = gi + fr * wi[r] - fi * wr[r]
                    gs[q, :, re] = gr
                    gs[q, :, im] = gi
                return carry

            return lax.fori_loop(0, group_pars // unroll, par_step, carry)

        lax.fori_loop(0, tiles, tile_step, 0)
        result = product(gs[...].reshape(group_rows, 2 * freq_pad), inv, 2 * freq_pad)
        for y in range(fast):
            gout[slot, y] = result[y * chunk : (y + 1) * chunk, :steps]

    y_sends, z_sends = {}, {}

    def pass_on(d):
        y_sends[d].wait_recv()
        z_out[d] = gout[d, my] + y_in[d]
        z_sends[d] = to_sensor(z_at(d) * fast + my, z_out.at[d], z_in.at[d], rz_s.at[d], rz_r.at[d])
        z_sends[d].start()

    order = list(range(slow - 1, -1, -1))
    for place, d in enumerate(order):
        adjoint_group(z_at(d), d)
        y_sends[d] = to_sensor(y_peer, gout.at[d, 1 - my], y_in.at[d], ry_s.at[d], ry_r.at[d])
        y_sends[d].start()
        if place:
            pass_on(order[place - 1])
    y_sends[0].wait_recv()
    answer = gout[0, my] + y_in[0]
    for d in order[:-1]:
        z_sends[d].wait_recv()
        answer = answer + z_in[d]
    out_ref[...] = answer

    own_y.wait_send()
    for d in range(1, slow):
        own_z[d].wait_send()
        forwards[d].wait_send()
        z_sends[d].wait_send()
    for d in range(slow):
        y_sends[d].wait_send()
    for j in range(1, n_param):
        sums[j].wait_send()
        spreads[j].wait_send()


def shards(n_sensor, n_param, parameter_field, operator_blocks, noise_weights):
    vecs, own_pars, steps = parameter_field.shape
    sens = noise_weights.shape[0]
    freqs = steps + 1
    flat_width = operator_blocks.shape[4]
    pars = flat_width // sens
    fast = 2
    slow = n_sensor // fast
    chunk = own_pars * vecs
    group_pars = fast * own_pars
    share = sens * vecs // n_param
    freq_pad = round_up(freqs, LANES)
    width_tiles = flat_width // LANES
    forward_table, inverse_table = tables(steps)
    field = jnp.transpose(parameter_field, (1, 0, 2)).reshape(chunk, steps)
    blocks = operator_blocks.reshape(2 * freqs * width_tiles, 1, LANES)
    sizes = (vecs, own_pars, steps, sens, pars, n_sensor, n_param, fast)
    raw_rows = round_up((freqs + freq_pad) * width_tiles, 8)
    vmem = pl.BlockSpec(memory_space=pltpu.VMEM)
    anywhere = pl.BlockSpec(memory_space=pl.ANY)
    dma = pltpu.SemaphoreType.DMA
    result = pl.pallas_call(
        functools.partial(kernel, sizes),
        out_shape=jax.ShapeDtypeStruct((chunk, steps), f32),
        in_specs=[vmem, anywhere, vmem, anywhere, anywhere],
        out_specs=vmem,
        scratch_shapes=[
            pltpu.VMEM((raw_rows, LANES), f32),
            pltpu.VMEM((2, pars, sens, freq_pad), f32),
            pltpu.VMEM(forward_table.shape, bf16),
            pltpu.VMEM(inverse_table.shape, bf16),
            pltpu.VMEM((n_sensor, chunk, steps), f32),
            pltpu.VMEM((group_pars, vecs, 2 * freq_pad), f32),
            pltpu.VMEM((sens, vecs, 2 * freq_pad), f32),
            pltpu.VMEM((n_param, share, steps), f32),
            pltpu.VMEM((n_param, share, steps), f32),
            pltpu.VMEM((n_param, share, steps), f32),
            pltpu.VMEM((n_param, share, steps), f32),
            pltpu.VMEM((group_pars, vecs, 2 * freq_pad), f32),
            pltpu.VMEM((slow, fast, chunk, steps), f32),
            pltpu.VMEM((slow, chunk, steps), f32),
            pltpu.VMEM((slow, chunk, steps), f32),
            pltpu.VMEM((slow, chunk, steps), f32),
            dma((3,)),
            dma((slow,)),
            dma((slow,)),
            dma((slow,)),
            dma((slow,)),
            dma((n_param,)),
            dma((n_param,)),
            dma((n_param,)),
            dma((n_param,)),
            dma((slow,)),
            dma((slow,)),
            dma((slow,)),
            dma((slow,)),
        ],
        compiler_params=pltpu.CompilerParams(
            collective_id=0, has_side_effects=True, vmem_limit_bytes=40 * 1024 * 1024
        ),
    )(field, blocks, noise_weights, jnp.asarray(forward_table), jnp.asarray(inverse_table))
    return jnp.transpose(result.reshape(own_pars, vecs, steps), (1, 0, 2))


def solution(mesh):
    in_specs = (
        P(None, ("param", "sensor"), None),
        P(None, None, "sensor", "param", None),
        P("sensor", None),
    )
    out_specs = P(None, ("param", "sensor"), None)
    run = functools.partial(shards, mesh.shape["sensor"], mesh.shape["param"])
    return jax.shard_map(run, mesh=mesh, in_specs=in_specs, out_specs=out_specs, check_vma=False)
```

profile of v0, /device:TPU:0, one launch (start us, length us, event | category | flops | bytes accessed | tf_op | source)
XLA Modules:
  0.0 51.8 jit_solution(16963254370734364555)
XLA Ops:
  0.0 0.0 copy-start
  0.0 1.6 %copy-done = bf16[2,1024,512]{2,1,0:T(8,128)(2,1)S(1)} copy-done((bf16[2,1024,512]{2,1,0:T(8,128)(2,1)S(1)}, bf16[2,1024,512]{2,1,0:T(8,128)(2,1)}, u32[]{:S(2)}) %copy-start) | copy-done | bytes 2097176
  1.6 0.0 copy-start.1
  1.6 1.6 %copy-done.1 = bf16[2,512,1024]{2,1,0:T(8,128)(2,1)S(1)} copy-done((bf16[2,512,1024]{2,1,0:T(8,128)(2,1)S(1)}, bf16[2,512,1024]{2,1,0:T(8,128)(2,1)}, u32[]{:S(2)}) %copy-start.1) | copy-done | bytes 2097176
  3.2 0.0 copy-start.2
  3.2 1.3 %copy-done.2 = f32[2,421,1,1,384]{4,3,2,1,0:T(1,128)S(1)} copy-done((f32[2,421,1,1,384]{4,3,2,1,0:T(1,128)S(1)}, f32[2,421,1,1,384]{4,3,2,1,0:T(1,128)}, u32[]{:S(2)}) %copy-start.2) | copy-done | bytes 1293336
  4.5 0.0 copy-start.3
  4.5 0.9 %copy-done.3 = f32[8,6,420]{2,0,1:T(8,128)S(1)} copy-done((f32[8,6,420]{2,0,1:T(8,128)S(1)}, f32[8,6,420]{2,0,1:T(8,128)}, u32[]{:S(2)}) %copy-start.3) | copy-done | bytes 80664
  5.4 0.0 copy-start.4
  5.4 0.7 %copy-done.4 = f32[8,420]{1,0:T(8,128)S(1)} copy-done((f32[8,420]{1,0:T(8,128)S(1)}, f32[8,420]{1,0:T(8,128)}, u32[]{:S(2)}) %copy-start.4) | copy-done | bytes 13464
  6.1 45.1 %shard_map.55 = f32[48,420]{1,0:T(8,128)S(1)} custom-call(f32[48,420]{1,0:T(8,128)S(1)} %bitcast.9, f32[2526,1,128]{2,1,0:T(1,128)S(1)} %bitcast.7, f32[8,420]{1,0:T(8,128)S(1)} %copy-done.4, bf16[2,512,1024]{2,1,0:T(8,128)(2,1)S(1)} %copy-done.1, bf16[2,1024,512]{2,1,0:T(8,128)(2,1)S(1)} %copy-done), custom_call_target="tpu_custom_call" | custom-call | tf_op jit(solution)/shard_map/pallas_call | solution.py:364
  51.2 0.6 %copy.7 = f32[8,6,420]{2,0,1:T(8,128)} copy(f32[8,6,420]{2,0,1:T(8,128)S(1)} %bitcast.8) | data formatting | bytes 161280
Async XLA Ops:
  0.0 1.6 %copy-start = (bf16[2,1024,512]{2,1,0:T(8,128)(2,1)S(1)}, bf16[2,1024,512]{2,1,0:T(8,128)(2,1)}, u32[]{:S(2)}) copy-start(bf16[2,1024,512]{2,1,0:T(8,128)(2,1)} %constant.5.clone.inv_hbm) | copy-start | bytes 6291460
  1.6 1.6 %copy-start.1 = (bf16[2,512,1024]{2,1,0:T(8,128)(2,1)S(1)}, bf16[2,512,1024]{2,1,0:T(8,128)(2,1)}, u32[]{:S(2)}) copy-start(bf16[2,512,1024]{2,1,0:T(8,128)(2,1)} %constant.4.clone.fwd_hbm) | copy-start | bytes 6291460
  3.2 1.3 %copy-start.2 = (f32[2,421,1,1,384]{4,3,2,1,0:T(1,128)S(1)}, f32[2,421,1,1,384]{4,3,2,1,0:T(1,128)}, u32[]{:S(2)}) copy-start(f32[2,421,1,1,384]{4,3,2,1,0:T(1,128)} %param.6) | copy-start | bytes 3879940
  4.5 0.9 %copy-start.3 = (f32[8,6,420]{2,0,1:T(8,128)S(1)}, f32[8,6,420]{2,0,1:T(8,128)}, u32[]{:S(2)}) copy-start(f32[8,6,420]{2,0,1:T(8,128)} %param.5) | copy-start | bytes 241924
  5.4 0.7 %copy-start.4 = (f32[8,420]{1,0:T(8,128)S(1)}, f32[8,420]{1,0:T(8,128)}, u32[]{:S(2)}) copy-start(f32[8,420]{1,0:T(8,128)} %weights_ref.1) | copy-start | bytes 40324
where the time goes:
time: 52.1 us; the launch traced here: 51.8 us
  Pallas kernels  45.1 us (87%)
  local copies, waits for them, and re-layouts  6.74 us (13%)
    pallas_call x1, Pallas kernels, shards(): pl.pallas_call(functools.partial(kernel, sizes), out_shape=jax.ShapeDtype...  45.1 us
    unnamed x11, local copies, waits for them, and re-layouts  6.74 us

commit v1 on v0

--- a/solution.py
+++ b/solution.py
@@ -57,6 +57,37 @@
     return dot(low, table_high) + dot(high, table_low) + dot(high, table_high)
 
 
+def packing(chunk, steps):
+    full, tail = steps // LANES, steps % LANES
+    folds = 1
+    if tail:
+        folds = max(f for f in range(1, LANES // tail + 1) if chunk % (8 * f) == 0 or f == 1)
+    tail_rows = chunk // folds if tail else 0
+    return full, tail, folds, tail_rows
+
+
+def pack_into(ref, value, chunk, steps):
+    full, tail, folds, tail_rows = packing(chunk, steps)
+    for c in range(full):
+        ref[c * chunk : (c + 1) * chunk] = value[:, c * LANES : (c + 1) * LANES]
+    if tail:
+        last = value[:, full * LANES :]
+        folded = last[:tail_rows]
+        for f in range(1, folds):
+            folded = folded + pltpu.roll(last[f * tail_rows : (f + 1) * tail_rows], f * tail, 1)
+        ref[full * chunk :] = folded
+
+
+def unpacked(value, chunk, steps):
+    full, tail, folds, tail_rows = packing(chunk, steps)
+    columns = [value[c * chunk : (c + 1) * chunk] for c in range(full)]
+    if tail:
+        folded = value[full * chunk :]
+        pieces = [folded] + [pltpu.roll(folded, LANES - f * tail, 1) for f in range(1, folds)]
+        columns.append(jnp.concatenate(pieces, axis=0))
+    return jnp.concatenate(columns, axis=1)
+
+
 def kernel(
     sizes,
     x_ref,
@@ -69,6 +100,7 @@
     ft,
     fwd,
     inv,
+    wide,
     xg,
     xs,
     ps,
@@ -83,6 +115,7 @@
     z_in,
     local_sem,
     gz_s,
+    gz_own,
     gz_r,
     gy_s,
     gy_r,
@@ -99,6 +132,7 @@
     slow = n_sensor // fast
     freqs = steps + 1
     freq_pad = round_up(freqs, LANES)
+    time_pad = round_up(steps, LANES)
     tiles = freq_pad // LANES
     group_pars = fast * own_pars
     chunk = own_pars * vecs
@@ -157,16 +191,33 @@
     load_fwd.start()
     load_inv = pltpu.make_async_copy(inv_hbm, inv, local_sem.at[2])
     load_inv.start()
+    wide[...] = jnp.zeros_like(wide)
+    wide[:, :steps] = x_ref[...]
+    pack_into(xg.at[me], wide[...], chunk, steps)
     pl.semaphore_wait(barrier, 1 + (slow - 1) + (n_param - 1))
 
-    own_y = to_sensor(y_peer, x_ref, xg.at[me], gy_s.at[0], gy_r.at[0])
-    own_y.start()
-    own_z = {}
-    for d in range(1, slow):
-        own_z[d] = to_sensor(z_at(d) * fast + my, x_ref, xg.at[me], gz_s.at[d], gz_r.at[d])
-        own_z[d].start()
-
-    xg[me] = x_ref[...]
+    def right_copy(source, send):
+        ref = xg.at[source * fast + my]
+        return to_sensor((mz + 1) * fast + my, ref, ref, send, gz_r.at[source])
+
+    def left_copy(source, send):
+        ref = xg.at[source * fast + my]
+        return to_sensor((mz - 1) * fast + my, ref, ref, send, gz_r.at[source])
+
+    def y_copy(source):
+        ref = xg.at[source * fast + my]
+        return to_sensor(y_peer, ref, ref, gy_s.at[source], gy_r.at[source])
+
+    @pl.when(mz + 1 < slow)
+    def _():
+        right_copy(mz, gz_s.at[mz]).start()
+
+    @pl.when(mz > 0)
+    def _():
+        left_copy(mz, gz_own.at[0]).start()
+
+    y_copy(mz).start()
+
     spread = jnp.concatenate(
         [jnp.broadcast_to(weights_ref[r : r + 1], (vecs, steps)) for r in range(sens)], axis=0
     )
@@ -186,14 +237,6 @@
                 per, sens, LANES
             )
 
-    forwards = {}
-
-    def forward_chunk(d):
-        own_z[d].wait_recv()
-        source = z_back(d) * fast + my
-        forwards[d] = to_sensor(y_peer, xg.at[source], xg.at[source], gy_s.at[d], gy_r.at[d])
-        forwards[d].start()
-
     load_blocks.wait()
 
     def turn_tile(tile, carry):
@@ -201,32 +244,24 @@
         turn(1, tile)
         return carry
 
-    ready = [d for d in range(1, slow)]
-    half = max(tiles // 2, 1)
-    lax.fori_loop(0, half, turn_tile, 0)
-    for d in ready[:1]:
-        forward_chunk(d)
-    lax.fori_loop(half, tiles, turn_tile, 0)
-    for d in ready[1:]:
-        forward_chunk(d)
+    lax.fori_loop(0, tiles, turn_tile, 0)
     load_fwd.wait()
 
     def lanes_of(tile, c):
         return pl.ds(pl.multiple_of(tile * LANES + c * freq_pad, LANES), LANES)
 
-    def forward_group(zz, initial):
-        field = xg[pl.ds(zz * fast, fast)].reshape(group_rows, steps)
-        xs[...] = product(field, fwd, steps).reshape(group_pars, vecs, 2 * freq_pad)
+    def forward_group(zz):
+        field = jnp.concatenate(
+            [unpacked(xg[zz * fast + y], chunk, steps) for y in range(fast)], axis=0
+        )
+        xs[...] = product(field, fwd, time_pad).reshape(group_pars, vecs, 2 * freq_pad)
         base = zz * group_pars
 
         def tile_step(tile, carry):
             re, im = lanes_of(tile, 0), lanes_of(tile, 1)
-            if initial:
-                acc = tuple(jnp.zeros((vecs, LANES), f32) for _ in range(2 * sens))
-            else:
-                acc = tuple(ps[r, :, re] for r in range(sens)) + tuple(
-                    ps[r, :, im] for r in range(sens)
-                )
+            acc = tuple(ps[r, :, re] for r in range(sens)) + tuple(
+                ps[r, :, im] for r in range(sens)
+            )
 
             def par_step(step, acc):
                 acc = list(acc)
@@ -248,12 +283,38 @@
 
         lax.fori_loop(0, tiles, tile_step, 0)
 
-    for d in range(slow):
-        if d == 0:
-            own_y.wait_recv()
-        else:
-            forwards[d].wait_recv()
-        forward_group(z_back(d), d == 0)
+    inner = jnp.minimum(mz, slow - 1 - mz)
+
+    def place_of(n):
+        near = (n + 1) // 2
+        left = jnp.where(n <= 2 * inner, n % 2 == 1, mz > inner)
+        distance = jnp.where(n <= 2 * inner, near, n - inner)
+        return jnp.where(left, mz - distance, mz + distance)
+
+    ps[...] = jnp.zeros_like(ps)
+
+    def gather_step(n, carry):
+        @pl.when(n + 1 < slow)
+        def _():
+            source = place_of(n + 1)
+            right_copy(source, gz_s.at[source]).wait_recv()
+
+            @pl.when((source < mz) & (mz + 1 < slow))
+            def _():
+                right_copy(source, gz_s.at[source]).start()
+
+            @pl.when((source > mz) & (mz > 0))
+            def _():
+                left_copy(source, gz_s.at[source]).start()
+
+            y_copy(source).start()
+
+        zz = place_of(n)
+        y_copy(zz).wait_recv()
+        forward_group(zz)
+        return carry
+
+    lax.fori_loop(0, slow, gather_step, 0)
 
     load_inv.wait()
     series = product(ps[...].reshape(rows, 2 * freq_pad), inv, 2 * freq_pad)
@@ -304,7 +365,7 @@
         lax.fori_loop(0, tiles, tile_step, 0)
         result = product(gs[...].reshape(group_rows, 2 * freq_pad), inv, 2 * freq_pad)
         for y in range(fast):
-            gout[slot, y] = result[y * chunk : (y + 1) * chunk, :steps]
+            pack_into(gout.at[slot, y], result[y * chunk : (y + 1) * chunk], chunk, steps)
 
     y_sends, z_sends = {}, {}
 
@@ -326,12 +387,27 @@
     for d in order[:-1]:
         z_sends[d].wait_recv()
         answer = answer + z_in[d]
-    out_ref[...] = answer
-
-    own_y.wait_send()
+    out_ref[...] = unpacked(answer, chunk, steps)[:, :steps]
+
+    @pl.when(mz > 0)
+    def _():
+        left_copy(mz, gz_own.at[0]).wait_send()
+
+    def drain(source, carry):
+        y_copy(source).wait_send()
+
+        @pl.when((source <= mz) & (mz + 1 < slow))
+        def _():
+            right_copy(source, gz_s.at[source]).wait_send()
+
+        @pl.when((source > mz) & (mz > 0))
+        def _():
+            left_copy(source, gz_s.at[source]).wait_send()
+
+        return carry
+
+    lax.fori_loop(0, slow, drain, 0)
     for d in range(1, slow):
-        own_z[d].wait_send()
-        forwards[d].wait_send()
         z_sends[d].wait_send()
     for d in range(slow):
         y_sends[d].wait_send()
@@ -357,6 +433,8 @@
     field = jnp.transpose(parameter_field, (1, 0, 2)).reshape(chunk, steps)
     blocks = operator_blocks.reshape(2 * freqs * width_tiles, 1, LANES)
     sizes = (vecs, own_pars, steps, sens, pars, n_sensor, n_param, fast)
+    full, _, _, tail_rows = packing(chunk, steps)
+    packed_rows = full * chunk + tail_rows
     raw_rows = round_up((freqs + freq_pad) * width_tiles, 8)
     vmem = pl.BlockSpec(memory_space=pltpu.VMEM)
     anywhere = pl.BlockSpec(memory_space=pl.ANY)
@@ -371,7 +449,8 @@
             pltpu.VMEM((2, pars, sens, freq_pad), f32),
             pltpu.VMEM(forward_table.shape, bf16),
             pltpu.VMEM(inverse_table.shape, bf16),
-            pltpu.VMEM((n_sensor, chunk, steps), f32),
+            pltpu.VMEM((chunk, round_up(steps, LANES)), f32),
+            pltpu.VMEM((n_sensor, packed_rows, LANES), f32),
             pltpu.VMEM((group_pars, vecs, 2 * freq_pad), f32),
             pltpu.VMEM((sens, vecs, 2 * freq_pad), f32),
             pltpu.VMEM((n_param, share, steps), f32),
@@ -379,12 +458,13 @@
             pltpu.VMEM((n_param, share, steps), f32),
             pltpu.VMEM((n_param, share, steps), f32),
             pltpu.VMEM((group_pars, vecs, 2 * freq_pad), f32),
-            pltpu.VMEM((slow, fast, chunk, steps), f32),
-            pltpu.VMEM((slow, chunk, steps), f32),
-            pltpu.VMEM((slow, chunk, steps), f32),
-            pltpu.VMEM((slow, chunk, steps), f32),
+            pltpu.VMEM((slow, fast, packed_rows, LANES), f32),
+            pltpu.VMEM((slow, packed_rows, LANES), f32),
+            pltpu.VMEM((slow, packed_rows, LANES), f32),
+            pltpu.VMEM((slow, packed_rows, LANES), f32),
             dma((3,)),
             dma((slow,)),
+            dma((1,)),
             dma((slow,)),
             dma((slow,)),
             dma((slow,)),
@@ -398,7 +478,7 @@
             dma((slow,)),
         ],
         compiler_params=pltpu.CompilerParams(
-            collective_id=0, has_side_effects=True, vmem_limit_bytes=40 * 1024 * 1024
+            collective_id=0, has_side_effects=True, vmem_limit_bytes=60 * 1024 * 1024
         ),
     )(field, blocks, noise_weights, jnp.asarray(forward_table), jnp.asarray(inverse_table))
     return jnp.transpose(result.reshape(own_pars, vecs, steps), (1, 0, 2))

time: 52.1 us -> 47.7 us (0.916)
  local copies, waits for them, and re-layouts: 6.74 us -> 1.54 us
  Pallas kernels: 45.1 us -> 45.9 us
    unnamed x11 -> x1, local copies, waits for them, and re-layouts: 6.74 us -> 1.54 us
    pallas_call x1, Pallas kernels: 45.1 us -> 45.9 us  [shards(): pl.pallas_call(functools.partial(kernel, sizes), out_shape=jax.ShapeDtype...]
where the time goes in v1:
time: 47.7 us; the launch traced here: 47.5 us
  Pallas kernels  45.9 us (96%)
  local copies, waits for them, and re-layouts  1.54 us (3%)
    pallas_call x1, Pallas kernels, shards(): pl.pallas_call(functools.partial(kernel, sizes), out_shape=jax.ShapeDtype...  45.9 us
    unnamed x1, local copies, waits for them, and re-layouts  1.54 us

profile of v1, /device:TPU:0, one launch (start us, length us, event | category | flops | bytes accessed | tf_op | source)
XLA Modules:
  0.0 47.5 jit_solution(16378301590150023013)
XLA Ops:
  0.0 45.9 %shard_map.55 = f32[48,420]{1,0:T(8,128)} custom-call(f32[48,420]{1,0:T(8,128)} %bitcast.9, f32[2526,1,128]{2,1,0:T(1,128)} %bitcast.7, f32[8,420]{1,0:T(8,128)} %weights_ref.1, bf16[2,512,1024]{2,1,0:T(8,128)(2,1)} %constant.4.clone.fwd_hbm, bf16[2,1024,512]{2,1,0:T(8,128)(2,1)} %constant.5.clone.inv_hbm), custom_call_target="tpu_custom_call" | custom-call | tf_op jit(solution)/shard_map/pallas_call | solution.py:442
  46.0 1.5 %copy.7 = f32[8,6,420]{2,0,1:T(8,128)} copy(f32[8,6,420]{2,0,1:T(8,128)} %bitcast.8) | data formatting | bytes 161280

commit v2 on v1

--- a/solution.py
+++ b/solution.py
@@ -139,6 +139,9 @@
     group_rows = group_pars * vecs
     rows = sens * vecs
     share = rows // n_param
+    packed_rows = xg.shape[1]
+    pieces = 2 if packed_rows % 16 == 0 else 1
+    piece_rows = packed_rows // pieces
     unroll = 4 if group_pars % 4 == 0 else 1
 
     me = lax.axis_index("sensor")
@@ -196,27 +199,36 @@
     pack_into(xg.at[me], wide[...], chunk, steps)
     pl.semaphore_wait(barrier, 1 + (slow - 1) + (n_param - 1))
 
-    def right_copy(source, send):
-        ref = xg.at[source * fast + my]
-        return to_sensor((mz + 1) * fast + my, ref, ref, send, gz_r.at[source])
-
-    def left_copy(source, send):
-        ref = xg.at[source * fast + my]
-        return to_sensor((mz - 1) * fast + my, ref, ref, send, gz_r.at[source])
-
-    def y_copy(source):
-        ref = xg.at[source * fast + my]
-        return to_sensor(y_peer, ref, ref, gy_s.at[source], gy_r.at[source])
-
-    @pl.when(mz + 1 < slow)
-    def _():
-        right_copy(mz, gz_s.at[mz]).start()
-
-    @pl.when(mz > 0)
-    def _():
-        left_copy(mz, gz_own.at[0]).start()
-
-    y_copy(mz).start()
+    def piece(h):
+        return pl.ds(h * piece_rows, piece_rows)
+
+    def right_copy(source, h):
+        ref = xg.at[source * fast + my, piece(h)]
+        slot = source * pieces + h
+        return to_sensor((mz + 1) * fast + my, ref, ref, gz_s.at[slot], gz_r.at[slot])
+
+    def left_copy(source, h, own=False):
+        ref = xg.at[source * fast + my, piece(h)]
+        slot = source * pieces + h
+        send = gz_own.at[h] if own else gz_s.at[slot]
+        return to_sensor((mz - 1) * fast + my, ref, ref, send, gz_r.at[slot])
+
+    def y_copy(source, h):
+        ref = xg.at[source * fast + my, piece(h)]
+        slot = source * pieces + h
+        return to_sensor(y_peer, ref, ref, gy_s.at[slot], gy_r.at[slot])
+
+    for h in range(pieces):
+
+        @pl.when(mz + 1 < slow)
+        def _():
+            right_copy(mz, h).start()
+
+        @pl.when(mz > 0)
+        def _():
+            left_copy(mz, h, True).start()
+
+        y_copy(mz, h).start()
 
     spread = jnp.concatenate(
         [jnp.broadcast_to(weights_ref[r : r + 1], (vecs, steps)) for r in range(sens)], axis=0
@@ -297,20 +309,22 @@
         @pl.when(n + 1 < slow)
         def _():
             source = place_of(n + 1)
-            right_copy(source, gz_s.at[source]).wait_recv()
-
-            @pl.when((source < mz) & (mz + 1 < slow))
-            def _():
-                right_copy(source, gz_s.at[source]).start()
-
-            @pl.when((source > mz) & (mz > 0))
-            def _():
-                left_copy(source, gz_s.at[source]).start()
-
-            y_copy(source).start()
+            for h in range(pieces):
+                right_copy(source, h).wait_recv()
+
+                @pl.when((source < mz) & (mz + 1 < slow))
+                def _():
+                    right_copy(source, h).start()
+
+                @pl.when((source > mz) & (mz > 0))
+                def _():
+                    left_copy(source, h).start()
+
+                y_copy(source, h).start()
 
         zz = place_of(n)
-        y_copy(zz).wait_recv()
+        for h in range(pieces):
+            y_copy(zz, h).wait_recv()
         forward_group(zz)
         return carry
 
@@ -370,47 +384,62 @@
     y_sends, z_sends = {}, {}
 
     def pass_on(d):
-        y_sends[d].wait_recv()
-        z_out[d] = gout[d, my] + y_in[d]
-        z_sends[d] = to_sensor(z_at(d) * fast + my, z_out.at[d], z_in.at[d], rz_s.at[d], rz_r.at[d])
-        z_sends[d].start()
+        for h in range(pieces):
+            y_sends[d, h].wait_recv()
+            z_out[d, piece(h)] = gout[d, my, piece(h)] + y_in[d, piece(h)]
+            slot = d * pieces + h
+            z_sends[d, h] = to_sensor(
+                z_at(d) * fast + my, z_out.at[d, piece(h)], z_in.at[d, piece(h)],
+                rz_s.at[slot], rz_r.at[slot],
+            )
+            z_sends[d, h].start()
 
     order = list(range(slow - 1, -1, -1))
     for place, d in enumerate(order):
         adjoint_group(z_at(d), d)
-        y_sends[d] = to_sensor(y_peer, gout.at[d, 1 - my], y_in.at[d], ry_s.at[d], ry_r.at[d])
-        y_sends[d].start()
-        if place:
-            pass_on(order[place - 1])
-    y_sends[0].wait_recv()
+        for h in range(pieces):
+            slot = d * pieces + h
+            y_sends[d, h] = to_sensor(
+                y_peer, gout.at[d, 1 - my, piece(h)], y_in.at[d, piece(h)],
+                ry_s.at[slot], ry_r.at[slot],
+            )
+            y_sends[d, h].start()
+        if place >= 2:
+            pass_on(order[place - 2])
+    if slow > 1:
+        pass_on(1)
+    for h in range(pieces):
+        y_sends[0, h].wait_recv()
     answer = gout[0, my] + y_in[0]
     for d in order[:-1]:
-        z_sends[d].wait_recv()
+        for h in range(pieces):
+            z_sends[d, h].wait_recv()
         answer = answer + z_in[d]
     out_ref[...] = unpacked(answer, chunk, steps)[:, :steps]
 
-    @pl.when(mz > 0)
-    def _():
-        left_copy(mz, gz_own.at[0]).wait_send()
+    for h in range(pieces):
+
+        @pl.when(mz > 0)
+        def _():
+            left_copy(mz, h, True).wait_send()
 
     def drain(source, carry):
-        y_copy(source).wait_send()
-
-        @pl.when((source <= mz) & (mz + 1 < slow))
-        def _():
-            right_copy(source, gz_s.at[source]).wait_send()
-
-        @pl.when((source > mz) & (mz > 0))
-        def _():
-            left_copy(source, gz_s.at[source]).wait_send()
+        for h in range(pieces):
+            y_copy(source, h).wait_send()
+
+            @pl.when((source <= mz) & (mz + 1 < slow))
+            def _():
+                right_copy(source, h).wait_send()
+
+            @pl.when((source > mz) & (mz > 0))
+            def _():
+                left_copy(source, h).wait_send()
 
         return carry
 
     lax.fori_loop(0, slow, drain, 0)
-    for d in range(1, slow):
-        z_sends[d].wait_send()
-    for d in range(slow):
-        y_sends[d].wait_send()
+    for copy in list(z_sends.values()) + list(y_sends.values()):
+        copy.wait_send()
     for j in range(1, n_param):
         sums[j].wait_send()
         spreads[j].wait_send()
@@ -463,19 +492,19 @@
             pltpu.VMEM((slow, packed_rows, LANES), f32),
             pltpu.VMEM((slow, packed_rows, LANES), f32),
             dma((3,)),
-            dma((slow,)),
-            dma((1,)),
-            dma((slow,)),
-            dma((slow,)),
-            dma((slow,)),
+            dma((2 * slow,)),
+            dma((2,)),
+            dma((2 * slow,)),
+            dma((2 * slow,)),
+            dma((2 * slow,)),
             dma((n_param,)),
             dma((n_param,)),
             dma((n_param,)),
             dma((n_param,)),
-            dma((slow,)),
-            dma((slow,)),
-            dma((slow,)),
-            dma((slow,)),
+            dma((2 * slow,)),
+            dma((2 * slow,)),
+            dma((2 * slow,)),
+            dma((2 * slow,)),
         ],
         compiler_params=pltpu.CompilerParams(
             collective_id=0, has_side_effects=True, vmem_limit_bytes=60 * 1024 * 1024

time: 47.7 us -> 45.6 us (0.956)
  Pallas kernels: 45.9 us -> 43.9 us
    pallas_call x1, Pallas kernels: 45.9 us -> 43.9 us  [shards(): pl.pallas_call(functools.partial(kernel, sizes), out_shape=jax.ShapeDtype...]
where the time goes in v2:
time: 45.6 us; the launch traced here: 45.4 us
  Pallas kernels  43.9 us (96%)
  local copies, waits for them, and re-layouts  1.54 us (3%)
    pallas_call x1, Pallas kernels, shards(): pl.pallas_call(functools.partial(kernel, sizes), out_shape=jax.ShapeDtype...  43.9 us
    unnamed x1, local copies, waits for them, and re-layouts  1.54 us

profile of v2, /device:TPU:0, one launch (start us, length us, event | category | flops | bytes accessed | tf_op | source)
XLA Modules:
  0.0 45.4 jit_solution(1519811942526714158)
XLA Ops:
  0.0 43.9 %shard_map.55 = f32[48,420]{1,0:T(8,128)} custom-call(f32[48,420]{1,0:T(8,128)} %bitcast.9, f32[2526,1,128]{2,1,0:T(1,128)} %bitcast.7, f32[8,420]{1,0:T(8,128)} %weights_ref.1, bf16[2,512,1024]{2,1,0:T(8,128)(2,1)} %constant.4.clone.fwd_hbm, bf16[2,1024,512]{2,1,0:T(8,128)(2,1)} %constant.5.clone.inv_hbm), custom_call_target="tpu_custom_call" | custom-call | tf_op jit(solution)/shard_map/pallas_call | solution.py:471
  43.9 1.5 %copy.7 = f32[8,6,420]{2,0,1:T(8,128)} copy(f32[8,6,420]{2,0,1:T(8,128)} %bitcast.8) | data formatting | bytes 161280
